TPU v7x, 1024 devices: a whole 8x8x8 slice. The times are simulated.
1024 devices in a mesh: dp: 128 (over y, z, core), expert: 8 (over x).
Axes of the slice: x: 8, y: 8, z: 8, core: 2. Of those that a mesh axis runs over, the one named last changes fastest.
Arguments:
- grad_partial: bfloat16 [8, 12, 256, 16384], P('expert', None, None, 'dp'), may hold values from -2.5 to 2.5
- momentum: float32 [16, 256, 16384], P('expert', None, 'dp'), may hold values from -12 to 12
- owner: int32 [12], replicated, may hold values from 0 to 7, as said below
Outputs:
- new_momentum: float32 [16, 256, 16384], P('expert', None, 'dp')
- update: float32 [12, 256, 16384], P(None, 'expert', 'dp')
Inputs may be any that keep to these rules, and one draw needn't show every extreme that they name: No owner index is named by more than 2 layers, and at least one is named by exactly 2.
All inputs are finite; a program needn't handle non-finite values.
Results may differ from a plain program's by a relative error of at most 0.0003.
Values sent between devices are 32-bit elements; how exact they have to be, the bound alone decides.
A program may use at most 128 MiB of HBM per device.

v0:
```python
import math

import jax
import jax.numpy as jnp
from jax import lax
from jax.sharding import PartitionSpec as P

N = 16384
CAP = 2
ITERS = 3


momentum_rate = 0.95
epsilon = 1e-07
quintic_one = 3.4445
quintic_two = -4.775
quintic_three = 2.0315
update_gain = 0.2


def slot_table(owner, slots):
    count = owner.shape[0]
    same_owner = owner[:, None] == owner[None, :]
    position = jnp.arange(count, dtype=jnp.int32)
    earlier = position[:, None] > position[None, :]
    rank = jnp.sum((same_owner & earlier).astype(jnp.int32), axis=1)
    slot_index = owner * CAP + rank
    return (slot_index[:, None] == jnp.arange(slots, dtype=jnp.int32)[None, :]).astype(jnp.float32)


def gram_sum(field):
    partial_gram = jnp.einsum("qrc,qtc->qrt", field, field, precision=lax.Precision.HIGHEST)
    return lax.psum(partial_gram, "dp")


def small_product(left, right):
    return jnp.einsum("qrt,qtu->qru", left, right, precision=lax.Precision.HIGHEST)


def on_device(grad_partial, momentum, owner):
    local = grad_partial[0]
    owners = lax.axis_size("expert")
    slots = owners * CAP
    select = slot_table(owner, slots)
    full_rows = local.shape[1]
    row_block = full_rows // owners
    columns = local.shape[2]
    summed = lax.psum_scatter(local.astype(jnp.float32), "expert", scatter_dimension=1, tiled=True)
    routed = jnp.einsum("lq,lrc->qrc", select, summed, precision=lax.Precision.HIGHEST)
    routed = routed.reshape(owners, CAP, row_block, columns)
    owned = lax.all_to_all(routed, "expert", split_axis=0, concat_axis=2, tiled=True)[0]
    new_momentum = momentum_rate * momentum + owned
    field = owned + momentum_rate * new_momentum
    squares = lax.psum(jnp.sum(field * field, axis=(1, 2)), "dp")
    field = field / (jnp.sqrt(squares) + epsilon)[:, None, None]
    gram = gram_sum(field)
    for step in range(ITERS):
        if step > 0:
            gram = gram_sum(field)
        square = small_product(gram, gram)
        mixer = quintic_two * gram + quintic_three * square
        field = quintic_one * field + jnp.einsum(
            "qrt,qtc->qrc", mixer, field, precision=lax.Precision.HIGHEST
        )
    result = update_gain * math.sqrt(N) * field
    returned = lax.all_to_all(
        result.reshape(CAP, owners, row_block, columns),
        "expert",
        split_axis=1,
        concat_axis=0,
        tiled=True,
    )
    update = jnp.einsum("lq,qrc->lrc", select, returned[:, 0], precision=lax.Precision.HIGHEST)
    return (new_momentum, update)


def solution(mesh):
    placed = (P("expert", None, None, "dp"), P("expert", None, "dp"), P())
    return jax.shard_map(
        on_device,
        mesh=mesh,
        in_specs=placed,
        out_specs=(P("expert", None, "dp"), P(None, "expert", "dp")),
        check_vma=False,
    )
```

profile of v0, /device:TPU:1, one launch (start us, length us, event | category | flops | bytes accessed | tf_op | source)
XLA Modules:
  0.0 969.3 jit_solution(17600375810964031555)
XLA Ops:
  7.2 0.0 copy-start.2
  7.2 0.0 reduce-scatter.2.cloned.1.call-start
  7.2 2.4 bitcast_convert_fusion
  9.6 0.0 copy-start.1
  9.7 0.0 reduce-scatter.2.cloned.1.call-update
  9.7 0.0 all-reduce.4.cloned.1.call-start
  9.7 0.0 copy-done.2
  9.7 0.2 convert_reduce_fusion
  9.9 55.5 %reduce-scatter.2.cloned.1.call-done = f32[12,32,128]{2,1,0:T(8,128)} async-done(((f32[12,256,128]{2,1,0:T(8,128)}), f32[12,32,128]{2,1,0:T(8,128)}) %reduce-scatter.2.cloned.1.call-update) | async-done | bytes 196624 | tf_op jit(solution)/shard_map/reduce_scatter | solution.py:48
  65.4 1.3 fusion.4
  66.8 0.1 copy.19
  66.9 13.8 %all_to_all.30 = f32[8,2,32,128]{3,1,2,0:T(2,128)S(1)} all-to-all(f32[8,2,32,128]{3,1,2,0:T(2,128)S(1)} %copy.19), channel_id=1, replica_groups=mesh['dp'=128,'expert'=8] {'expert'}, dimensions={0} | all-to-all | bytes 524288 | tf_op jit(solution)/shard_map/all_to_all | solution.py:51
  80.7 0.0 copy-done.1
  80.7 0.2 multiply_reduce_fusion
  80.9 0.0 copy-start
  80.9 254.0 %psum.28 = f32[2]{0:T(128)S(1)} all-reduce(f32[2]{0:T(128)S(1)} %get-tuple-element.8), channel_id=1, replica_groups=mesh['dp'=128,'expert'=8] {'dp'}, use_global_device_ids=true, to_apply=%region_3.0 | all-reduce | flops 2 | bytes 16 | tf_op jit(solution)/shard_map/psum | solution.py:54
  334.8 1.5 fusion.13
  336.3 0.0 all-reduce.4.cloned.1.call-update
  336.3 0.0 all-reduce.6.cloned.1.call-start
  336.4 193.4 %all-reduce.4.cloned.1.call-done = f32[2,256,256]{2,1,0:T(8,128)} async-done(((f32[2,256,256]{2,1,0:T(8,128)}), f32[2,256,256]{2,1,0:T(8,128)}) %all-reduce.4.cloned.1.call-update) | async-done | bytes 524304 | tf_op jit(solution)/shard_map/psum | solution.py:33
  529.8 2.1 fusion.2
  531.8 0.0 copy-done
  531.9 0.7 convolution_add_fusion.2
  532.5 1.4 fusion.14
  533.9 0.0 all-reduce.6.cloned.1.call-update
  533.9 0.0 all-reduce.8.cloned.1.call-start
  534.0 202.5 %all-reduce.6.cloned.1.call-done = f32[2,256,256]{2,1,0:T(8,128)} async-done(((f32[2,256,256]{2,1,0:T(8,128)}), f32[2,256,256]{2,1,0:T(8,128)}) %all-reduce.6.cloned.1.call-update) | async-done | bytes 524304 | tf_op jit(solution)/shard_map/psum | solution.py:33
  736.5 2.1 fusion.1
  738.6 0.6 convolution_add_fusion.1
  739.2 1.4 fusion.15
  740.6 0.0 all-reduce.8.cloned.1.call-update
  740.6 202.5 %all-reduce.8.cloned.1.call-done = f32[2,256,256]{2,1,0:T(8,128)} async-done(((f32[2,256,256]{2,1,0:T(8,128)}), f32[2,256,256]{2,1,0:T(8,128)}) %all-reduce.8.cloned.1.call-update) | async-done | bytes 524304 | tf_op jit(solution)/shard_map/psum | solution.py:33
  943.1 2.1 fusion
  945.2 0.6 fusion.3
  945.9 15.6 %all_to_all.31 = f32[2,8,32,128]{3,2,0,1:T(8,128)S(1)} all-to-all(f32[2,8,32,128]{3,2,0,1:T(8,128)S(1)} %copy.21), channel_id=1, replica_groups=mesh['dp'=128,'expert'=8] {'expert'}, dimensions={1} | all-to-all | bytes 524288 | tf_op jit(solution)/shard_map/all_to_all | solution.py:66
  961.5 0.2 copy.22
  961.7 0.3 fusion.8
  962.0 0.7 copy.23
  (4 shorter events, 0.1 us)
Async XLA Ops:
  7.2 2.6 copy-start.2
  7.2 58.3 %reduce-scatter.2.cloned.1.call-start = ((), (), s32[]{:S(2)}) async-start(), calls=%async_computation.3 | async-start | bytes 1769472 | tf_op jit(solution)/shard_map/reduce_scatter | solution.py:48
  9.6 71.1 %copy-start.1 = (f32[2,256,128]{2,1,0:T(8,128)S(1)}, f32[2,256,128]{2,1,0:T(8,128)}, u32[]{:S(2)}) copy-start(f32[2,256,128]{2,1,0:T(8,128)} %param.4) | copy-start | bytes 786436
  9.7 520.1 %all-reduce.4.cloned.1.call-start = ((), (), s32[]{:S(2)}) async-start(), calls=%async_computation.4 | async-start | bytes 1048576 | tf_op jit(solution)/shard_map/psum | solution.py:33
  80.9 451.0 %copy-start = (f32[2,256,128]{2,1,0:T(8,128)}, f32[2,256,128]{2,1,0:T(8,128)S(1)}, u32[]{:S(2)}) copy-start(f32[2,256,128]{2,1,0:T(8,128)S(1)} %get-tuple-element.9) | copy-start | bytes 786436
  336.3 400.1 %all-reduce.6.cloned.1.call-start = ((), (), s32[]{:S(2)}) async-start(), calls=%async_computation.5 | async-start | bytes 1048576 | tf_op jit(solution)/shard_map/psum | solution.py:33
  533.9 409.2 %all-reduce.8.cloned.1.call-start = ((), (), s32[]{:S(2)}) async-start(), calls=%async_computation.6 | async-start | bytes 1048576 | tf_op jit(solution)/shard_map/psum | solution.py:33
Sparse Core Ops, SparseCore 0:
  11.4 53.9 reduce-scatter.1
  336.5 193.2 all-reduce.3
  534.1 202.3 all-reduce.5
  740.7 202.3 all-reduce.7
where the time goes:
time: 973 us; the launch traced here: 969 us
  waiting for transfers between devices  654 us (67%)
  blocking collectives  283 us (29%)
  matrix products  14.1 us (1%)
  between operations  13.9 us (1%)
    psum x3, waiting for transfers between devices, gram_sum(): return lax.psum(partial_gram, 'dp')  598 us
    psum x1, blocking collectives, on_device(): squares = lax.psum(jnp.sum(field * field, axis=(1, 2)), 'dp')  254 us
    reduce_scatter x1, waiting for transfers between devices, on_device(): lax.psum_scatter(local.astype(jnp.float32), 'expert', scatter_dimension=1...  55.5 us
  transfers between devices with their start and end apart: 4, of which 4 were waited for; matrix products, arithmetic and copies ran while one was open for 0% of the time, Pallas kernels for 0%

commit v1 on v0

v1 whole, which is shorter than its diff:
```python
import functools
import math

import jax
import jax.numpy as jnp
from jax import lax
from jax.experimental import pallas as pl
from jax.experimental.pallas import tpu as pltpu
from jax.sharding import PartitionSpec as P

N = 16384
CAP = 2
OWNERS = 8
LAYERS = 12
ROWS = 256
COLS = 128
HALF = ROWS // 2
BLOCK = ROWS // OWNERS
PIECE = 3 * HALF // 16

momentum_rate = 0.95
epsilon = 1e-07
quintic_one = 3.4445
quintic_two = -4.775
quintic_three = 2.0315
update_gain = 0.2

MESH = pl.DeviceIdType.MESH
FAR_FIRST = (4, 3, 5, 2, 6, 1, 7)
STEPS = 4


def split(value):
    high = value.astype(jnp.bfloat16)
    low = (value - high.astype(jnp.float32)).astype(jnp.bfloat16)
    return high, low


def dot(left, right, dims):
    return lax.dot_general(left, right, (dims, ((), ())), preferred_element_type=jnp.float32)


def product(left, right, dims=((1,), (0,))):
    cross = dot(left[0], right[1], dims) + dot(left[1], right[0], dims)
    return dot(left[0], right[0], dims) + cross


def mod8(value):
    return lax.rem(value + 16, 8)


def kernel(
    owner_ref,
    grad_hbm,
    momentum_hbm,
    new_momentum_ref,
    update_ref,
    grad_ref,
    momentum_ref,
    first_ref,
    chain_ref,
    field_ref,
    pair_ref,
    gram_ref,
    early_ref,
    early_sum_ref,
    late_ref,
    late_sum_ref,
    whole_ref,
    result_ref,
    rows_ref,
    load_sem,
    chain_send,
    chain_recv,
    pair_send,
    pair_recv,
    gram_send,
    gram_recv,
    rows_send,
    rows_recv,
    go_left,
    go_right,
    go_core,
    go_y,
    go_z,
    go_x,
):
    place = lax.axis_index("dp")
    x = lax.axis_index("expert")
    y, z, core = place // 16, lax.rem(place // 2, 8), lax.rem(place, 2)

    def device(y_, z_, core_, x_):
        return ((y_ * 8 + z_) * 2 + core_, x_)

    def signal(sem, target):
        pl.semaphore_signal(sem, inc=1, device_id=target, device_id_type=MESH)

    def each(low, high, body):
        def step(index, carry):
            body(index)
            return carry

        lax.fori_loop(low, high, step, 0)

    def await_all(sem, count):
        @pl.when(count > 0)
        def _():
            pl.semaphore_wait(sem, count)

    barrier = pltpu.get_barrier_semaphore()

    def greet_x(j):
        signal(barrier, device(y, z, 0, j))
        signal(barrier, device(y, z, 1, j))

    each(0, x, greet_x)
    each(0, y, lambda j: signal(barrier, device(j, z, core, x)))
    each(0, z, lambda j: signal(barrier, device(y, j, core, x)))
    each(0, core, lambda j: signal(barrier, device(y, z, j, x)))

    load_grad = pltpu.make_async_copy(grad_hbm.at[0], grad_ref, load_sem.at[0])
    load_momentum = pltpu.make_async_copy(momentum_hbm, momentum_ref, load_sem.at[1])
    load_grad.start()
    load_momentum.start()

    owners = [owner_ref[layer] for layer in range(LAYERS)]
    layers = []
    for ahead in range(OWNERS):
        wanted = mod8(x + ahead)
        first = jnp.int32(-1)
        second = jnp.int32(-1)
        for layer in range(LAYERS):
            hit = owners[layer] == wanted
            second = jnp.where(hit & (first >= 0), layer, second)
            first = jnp.where(hit & (first < 0), layer, first)
        layers.append((first, second))

    def share(ahead, slot, half):
        layer = layers[ahead % 8][slot]
        value = grad_ref[jnp.maximum(layer, 0), pl.ds(half * HALF, HALF), :].astype(jnp.float32)
        return jnp.where(layer >= 0, value, 0.0)

    load_grad.wait()
    await_all(barrier, 2 * (7 - x) + (7 - y) + (7 - z) + (1 - core))

    @pl.when(x < 7)
    def _():
        signal(go_left, device(y, z, core, x + 1))

    @pl.when(x == 0)
    def _():
        signal(go_right, device(y, z, core, 7))

    def go_ahead():
        each(core + 1, 2, lambda j: signal(go_core, device(y, z, j, x)))
        each(y + 1, 8, lambda j: signal(go_y, device(j, z, core, x)))
        each(z + 1, 8, lambda j: signal(go_z, device(y, j, core, x)))

        def go_to_x(j):
            signal(go_x, device(y, z, 0, j))
            signal(go_x, device(y, z, 1, j))

        each(x + 1, 8, go_to_x)

    def chain_index(direction, slot, half):
        return (direction * 2 + slot) * 2 + half

    def chain_copy(direction, slot, half, step):
        index = chain_index(direction, slot, half)
        source = first_ref.at[index] if step == 0 else chain_ref.at[index * STEPS + step - 1]
        target = mod8(x + 1) if direction == 0 else mod8(x + 7)
        return pltpu.make_async_remote_copy(
            src_ref=source,
            dst_ref=chain_ref.at[index * STEPS + step],
            send_sem=chain_send.at[index * STEPS + step],
            recv_sem=chain_recv.at[index * STEPS + step],
            device_id=device(y, z, core, target),
            device_id_type=MESH,
        )

    started = []
    for step in range(STEPS):
        for length in (4, 3):
            if step >= length:
                continue
            for slot in range(CAP):
                for direction in (0, 1):
                    half = 0 if (direction == 0) == (length == 4) else 1
                    ahead = length - step if direction == 0 else step - length
                    index = chain_index(direction, slot, half)
                    if step == 0:
                        first_ref[index] = share(ahead, slot, half)
                        if length == 4 and slot == 0:
                            if direction == 0:
                                each(0, (x == 7).astype(jnp.int32), lambda j: pl.semaphore_wait(go_right, 1))
                            else:
                                each(0, (x > 0).astype(jnp.int32), lambda j: pl.semaphore_wait(go_left, 1))
                    else:
                        chain_copy(direction, slot, half, step - 1).wait_recv()
                        at = index * STEPS + step - 1
                        chain_ref[at] = chain_ref[at] + share(ahead, slot, half)
                    copy = chain_copy(direction, slot, half, step)
                    copy.start()
                    started.append(copy)
        if step == 0:
            go_ahead()
            load_momentum.wait()

    for half in range(2):
        rows = pl.ds(half * HALF, HALF)
        for slot in range(CAP):
            lengths = (4, 3) if half == 0 else (3, 4)
            total = share(0, slot, half)
            for direction in (0, 1):
                last = lengths[direction] - 1
                chain_copy(direction, slot, half, last).wait_recv()
                total = total + chain_ref[chain_index(direction, slot, half) * STEPS + last]
            fresh = momentum_rate * momentum_ref[slot, rows, :] + total
            new_momentum_ref[slot, rows, :] = fresh
            field_ref[slot, rows, :] = total + momentum_rate * fresh

    each(0, core, lambda j: pl.semaphore_wait(go_core, 1))
    pair = pltpu.make_async_remote_copy(
        src_ref=field_ref.at[1 - core],
        dst_ref=pair_ref,
        send_sem=pair_send,
        recv_sem=pair_recv,
        device_id=device(y, z, 1 - core, x),
        device_id_type=MESH,
    )
    pair.start()
    started.append(pair)
    mine = field_ref[core]
    mine_split = split(mine)
    rows_rows = ((1,), (1,))
    gram = product(mine_split, mine_split, rows_rows)
    pair.wait_recv()
    other = pair_ref[...]
    other_split = split(other)
    gram = gram + product(other_split, other_split, rows_rows)

    stacked = jnp.concatenate([gram[:HALF, :HALF], gram[:HALF, HALF:], gram[HALF:, HALF:]], axis=0)
    gram_ref[...] = stacked.reshape(16, PIECE, HALF)
    await_all(go_y, y)
    await_all(go_z, z)

    def along(axis, ahead):
        return device(mod8(y + ahead), z, core, x) if axis == 0 else device(y, mod8(z + ahead), core, x)

    where = (y, z)

    def gram_copy(stage, order, ahead):
        axis = 1 - order if stage == 1 else order
        if stage == 0:
            source, target = gram_ref.at[order * 8 + mod8(where[order] + ahead)], early_ref.at[order, ahead - 1]
        elif stage == 1:
            source, target = early_sum_ref.at[order], late_ref.at[order, ahead - 1]
        else:
            source, target = late_sum_ref.at[order], whole_ref.at[order * 8 + where[order]]
        index = (stage * 2 + order) * 7 + ahead - 1
        return pltpu.make_async_remote_copy(
            src_ref=source,
            dst_ref=target,
            send_sem=gram_send.at[index],
            recv_sem=gram_recv.at[index],
            device_id=along(axis, ahead),
            device_id_type=MESH,
        )

    def gram_arrival(stage, order, ahead):
        if stage < 2:
            gram_copy(stage, order, ahead).wait_recv()
            return
        index = (stage * 2 + order) * 7 + ahead - 1
        pltpu.make_async_remote_copy(
            src_ref=late_sum_ref.at[order],
            dst_ref=whole_ref.at[order * 8 + mod8(where[order] - ahead)],
            send_sem=gram_send.at[index],
            recv_sem=gram_recv.at[index],
            device_id=along(order, ahead),
            device_id_type=MESH,
        ).wait_recv()

    for stage in range(3):
        if stage == 1:
            for order in range(2):
                total = gram_ref[order * 8 + where[order]]
                for ahead in range(1, 8):
                    gram_arrival(0, order, ahead)
                    total = total + early_ref[order, ahead - 1]
                early_sum_ref[order] = total
        if stage == 2:
            for order in range(2):
                total = early_sum_ref[order]
                for ahead in range(1, 8):
                    gram_arrival(1, order, ahead)
                    total = total + late_ref[order, ahead - 1]
                late_sum_ref[order] = total
                whole_ref[order * 8 + where[order]] = total
        for ahead in FAR_FIRST:
            for order in range(2):
                copy = gram_copy(stage, order, ahead)
                copy.start()
                started.append(copy)
    for order in range(2):
        for ahead in range(1, 8):
            gram_arrival(2, order, ahead)

    blocks = whole_ref[...].reshape(3 * HALF, HALF)
    corner, side, rest = blocks[:HALF], blocks[HALF : 2 * HALF], blocks[2 * HALF :]
    row = lax.broadcasted_iota(jnp.int32, (HALF, HALF), 0)
    column = lax.broadcasted_iota(jnp.int32, (HALF, HALF), 1)
    diagonal = jnp.where(row == column, corner + rest, 0.0)
    squares = jnp.sum(diagonal)
    scale = 1.0 / (jnp.sqrt(jnp.full((1, 1), squares, jnp.float32)) + epsilon)
    gram = jnp.concatenate(
        [jnp.concatenate([corner, side], axis=1), jnp.concatenate([side.T, rest], axis=1)], axis=0
    )
    gram = gram * (scale * scale)
    field = jnp.concatenate([mine * scale, other * scale], axis=1)

    for step in range(2):
        gram_split = split(gram)
        square = product(gram_split, gram_split)
        square_split = split(square)
        cube = product(gram_split, square_split)
        mixer = quintic_two * gram + quintic_three * square
        mixed = quintic_one * gram + quintic_two * square + quintic_three * cube
        mixer_split = split(mixer)
        field = quintic_one * field + product(mixer_split, split(field))
        gram = quintic_one * mixed + product(split(mixed), mixer_split)
    gram_split = split(gram)
    bent = product(gram_split, split(field))
    twice = product(gram_split, split(bent))
    gain = update_gain * math.sqrt(N)
    result = (gain * quintic_one) * field + (gain * quintic_two) * bent + (gain * quintic_three) * twice

    result_ref[0] = result[:, :COLS]
    result_ref[1] = result[:, COLS:]
    await_all(go_x, 2 * x)

    def rows_copy(ahead, other_core):
        target = mod8(x + ahead)
        index = other_core * 8 + ahead
        return pltpu.make_async_remote_copy(
            src_ref=result_ref.at[other_core, pl.ds(pl.multiple_of(target * BLOCK, BLOCK), BLOCK), :],
            dst_ref=rows_ref.at[x * 2 + core],
            send_sem=rows_send.at[index],
            recv_sem=rows_recv.at[index],
            device_id=device(y, z, core if other_core == 0 else 1 - core, target),
            device_id_type=MESH,
        )

    def rows_arrival(ahead, other_core):
        source = mod8(x - ahead)
        from_core = core if other_core == 0 else 1 - core
        index = other_core * 8 + ahead
        pltpu.make_async_remote_copy(
            src_ref=result_ref.at[other_core, pl.ds(0, BLOCK), :],
            dst_ref=rows_ref.at[source * 2 + from_core],
            send_sem=rows_send.at[index],
            recv_sem=rows_recv.at[index],
            device_id=device(y, z, from_core, mod8(x + ahead)),
            device_id_type=MESH,
        ).wait_recv()

    partners = [(ahead, other_core) for ahead in FAR_FIRST for other_core in range(2)] + [(0, 1)]
    for ahead, other_core in partners:
        copy = rows_copy(ahead, other_core)
        copy.start()
        started.append(copy)
    rows_ref[x * 2 + core] = result_ref[0, pl.ds(pl.multiple_of(x * BLOCK, BLOCK), BLOCK), :]
    slots = []
    for layer in range(LAYERS):
        rank = jnp.int32(0)
        for before in range(layer):
            rank = rank + (owners[before] == owners[layer]).astype(jnp.int32)
        slots.append(owners[layer] * CAP + rank)
    for ahead, other_core in partners:
        rows_arrival(ahead, other_core)
    for layer in range(LAYERS):
        update_ref[layer] = rows_ref[slots[layer]]
    for copy in started:
        copy.wait_send()


def on_device(grad_partial, momentum, owner):
    f32 = jnp.float32
    chains = 8 * STEPS
    dma = pltpu.SemaphoreType.DMA
    regular = pltpu.SemaphoreType.REGULAR
    return pl.pallas_call(
        kernel,
        out_shape=(
            jax.ShapeDtypeStruct((CAP, ROWS, COLS), f32),
            jax.ShapeDtypeStruct((LAYERS, BLOCK, COLS), f32),
        ),
        in_specs=[
            pl.BlockSpec(memory_space=pltpu.SMEM),
            pl.BlockSpec(memory_space=pl.ANY),
            pl.BlockSpec(memory_space=pl.ANY),
        ],
        out_specs=[pl.BlockSpec(memory_space=pltpu.VMEM)] * 2,
        scratch_shapes=[
            pltpu.VMEM((LAYERS, ROWS, COLS), jnp.bfloat16),
            pltpu.VMEM((CAP, ROWS, COLS), f32),
            pltpu.VMEM((8, HALF, COLS), f32),
            pltpu.VMEM((chains, HALF, COLS), f32),
            pltpu.VMEM((CAP, ROWS, COLS), f32),
            pltpu.VMEM((ROWS, COLS), f32),
            pltpu.VMEM((16, PIECE, HALF), f32),
            pltpu.VMEM((2, 7, PIECE, HALF), f32),
            pltpu.VMEM((2, PIECE, HALF), f32),
            pltpu.VMEM((2, 7, PIECE, HALF), f32),
            pltpu.VMEM((2, PIECE, HALF), f32),
            pltpu.VMEM((16, PIECE, HALF), f32),
            pltpu.VMEM((2, ROWS, COLS), f32),
            pltpu.VMEM((OWNERS * CAP, BLOCK, COLS), f32),
            dma((2,)),
            dma((chains,)),
            dma((chains,)),
            dma,
            dma,
            dma((42,)),
            dma((42,)),
            dma((16,)),
            dma((16,)),
            regular,
            regular,
            regular,
            regular,
            regular,
            regular,
        ],
        compiler_params=pltpu.CompilerParams(
            collective_id=0, has_side_effects=True, vmem_limit_bytes=63 * 1024 * 1024
        ),
    )(owner, grad_partial, momentum)


def solution(mesh):
    placed = (P("expert", None, None, "dp"), P("expert", None, "dp"), P())
    return jax.shard_map(
        on_device,
        mesh=mesh,
        in_specs=placed,
        out_specs=(P("expert", None, "dp"), P(None, "expert", "dp")),
        check_vma=False,
    )
```

time: 973 us -> 78.2 us (0.08)
  waiting for transfers between devices: 654 us -> 0 us
  blocking collectives: 283 us -> 0 us
  Pallas kernels: 0 us -> 74.9 us
  matrix products: 14.1 us -> 0 us
  between operations: 13.9 us -> 0.65 us
    psum x3 -> x0, waiting for transfers between devices: 598 us -> none  [gram_sum(): return lax.psum(partial_gram, 'dp')]
    psum x1 -> x0, blocking collectives: 254 us -> none  [on_device(): squares = lax.psum(jnp.sum(field * field, axis=(1, 2)), 'dp')]
    pallas_call x0 -> x1, Pallas kernels: none -> 74.9 us  [on_device(): pl.pallas_call(kernel, out_shape=(jax.ShapeDtypeStruct((CAP, ROWS, COLS),...]
    reduce_scatter x1 -> x0, waiting for transfers between devices: 55.5 us -> none  [on_device(): lax.psum_scatter(local.astype(jnp.float32), 'expert', scatter_dimension=1...]
    all_to_all x2 -> x0, blocking collectives: 29.4 us -> none  [the longest x1 15.6 us: on_device(): lax.all_to_all(result.reshape(CAP, owners, row_block, columns), 'expert',...]
    dot_general x11 -> x0, matrix products: 14.1 us -> none  [the longest x3 6.25 us: small_product(): jnp.einsum('qrt,qtu->qru', left, right, precision=lax.Precision.HIGHEST)]
  transfers between devices with their start and end apart: 4 -> 0, of which waited for: 4 -> 0; matrix products, arithmetic and copies ran while one was open for 0% -> 0% of each run, Pallas kernels for 0% -> 0%
where the time goes in v1:
time: 78.2 us; the launch traced here: 78 us
  Pallas kernels  74.9 us (96%)
  local copies, waits for them, and re-layouts  2.39 us (3%)
    pallas_call x1, Pallas kernels, on_device(): pl.pallas_call(kernel, out_shape=(jax.ShapeDtypeStruct((CAP, ROWS, COLS),...  74.9 us
    unnamed x4, local copies, waits for them, and re-layouts  2.39 us

profile of v1, /device:TPU:1, one launch (start us, length us, event | category | flops | bytes accessed | tf_op | source)
XLA Modules:
  0.0 78.0 jit_solution(6351147034770201872)
XLA Ops:
  0.6 74.9 %shard_map.50 = (f32[2,256,128]{2,1,0:T(8,128)}, f32[12,32,128]{2,1,0:T(8,128)}) custom-call(s32[12]{0:T(128)} %owner_ref.1, bf16[1,12,256,128]{3,2,1,0:T(8,128)(2,1)} %grad_hbm.1, f32[2,256,128]{2,1,0:T(8,128)} %momentum_hbm.1), custom_call_target="tpu_custom_call" | custom-call | tf_op jit(solution)/shard_map/pallas_call | solution.py:392
  75.6 0.0 copy-start
  75.6 1.7 %copy.7 = f32[2,256,128]{2,1,0:T(8,128)} copy(f32[2,256,128]{2,1,0:T(8,128)} %get-tuple-element.4) | data formatting | bytes 524288
  77.3 0.0 copy-done
  77.3 0.7 copy.8
Async XLA Ops:
  75.6 1.7 %copy-start = (f32[12,32,128]{2,1,0:T(8,128)S(1)}, f32[12,32,128]{2,1,0:T(8,128)}, u32[]{:S(2)}) copy-start(f32[12,32,128]{2,1,0:T(8,128)} %get-tuple-element.5) | copy-start | bytes 589828

commit v2 on v1

v2 whole, which is shorter than its diff:
```python
import functools
import math

import jax
import jax.numpy as jnp
from jax import lax
from jax.experimental import pallas as pl
from jax.experimental.pallas import tpu as pltpu
from jax.sharding import PartitionSpec as P

N = 16384
CAP = 2
OWNERS = 8
LAYERS = 12
ROWS = 256
COLS = 128
HALF = ROWS // 2
BLOCK = ROWS // OWNERS
TILE = ROWS // 16
PIECE = TILE + 1

momentum_rate = 0.95
epsilon = 1e-07
quintic_one = 3.4445
quintic_two = -4.775
quintic_three = 2.0315
update_gain = 0.2

MESH = pl.DeviceIdType.MESH
FAR_FIRST = (4, 3, 5, 2, 6, 1, 7)
STEPS = 4
PARTS = (slice(0, HALF), slice(HALF, ROWS))


def split(value):
    high = value.astype(jnp.bfloat16)
    low = (value - high.astype(jnp.float32)).astype(jnp.bfloat16)
    return high, low


def dot(left, right, dims):
    return lax.dot_general(left, right, (dims, ((), ())), preferred_element_type=jnp.float32)


def product(left, right, dims=((1,), (0,))):
    cross = dot(left[0], right[1], dims) + dot(left[1], right[0], dims)
    return dot(left[0], right[0], dims) + cross


def mod8(value):
    return lax.rem(value + 16, 8)


def kernel(
    owner_hbm,
    grad_hbm,
    momentum_hbm,
    owned_hbm,
    update_hbm,
    owner_ref,
    grad_ref,
    momentum_ref,
    first_ref,
    chain_ref,
    owned_ref,
    field_ref,
    pair_ref,
    base_out_ref,
    base_ref,
    back_out_ref,
    back_ref,
    last_ref,
    gram_ref,
    early_ref,
    early_sum_ref,
    late_ref,
    late_sum_ref,
    whole_ref,
    result_ref,
    rows_ref,
    update_ref,
    load_sem,
    chain_send,
    chain_recv,
    last_recv,
    pair_send,
    pair_recv,
    gram_send,
    gram_recv,
    rows_send,
    rows_recv,
):
    place = lax.axis_index("dp")
    x = lax.axis_index("expert")
    y, z, core = place // 16, lax.rem(place // 2, 8), lax.rem(place, 2)

    def device(y_, z_, core_, x_):
        return ((y_ * 8 + z_) * 2 + core_, x_)

    def signal(sem, target):
        pl.semaphore_signal(sem, inc=1, device_id=target, device_id_type=MESH)

    barrier = pltpu.get_barrier_semaphore()

    for ahead in (1, 7, 2, 6, 3, 5, 4):
        for other in range(2):
            signal(barrier, device(y, z, other, mod8(x + ahead)))
    for ahead in range(1, 8):
        signal(barrier, device(mod8(y + ahead), z, core, x))
        signal(barrier, device(y, mod8(z + ahead), core, x))
    signal(barrier, device(y, z, 1 - core, x))

    load_grad = pltpu.make_async_copy(grad_hbm.at[0], grad_ref, load_sem.at[0])
    load_momentum = pltpu.make_async_copy(momentum_hbm, momentum_ref, load_sem.at[1])
    load_owner = pltpu.make_async_copy(owner_hbm, owner_ref, load_sem.at[2])
    load_owner.start()
    load_grad.start()
    load_momentum.start()

    load_owner.wait()
    owners = [owner_ref[layer] for layer in range(LAYERS)]
    layers = []
    for ahead in range(OWNERS):
        wanted = mod8(x + ahead)
        first = jnp.int32(-1)
        second = jnp.int32(-1)
        for layer in range(LAYERS):
            hit = owners[layer] == wanted
            second = jnp.where(hit & (first >= 0), layer, second)
            first = jnp.where(hit & (first < 0), layer, first)
        layers.append((first, second))

    def share(ahead, slot, part):
        first, second = layers[ahead % 8]
        layer = jnp.where(slot == 0, first, second)
        value = grad_ref[jnp.maximum(layer, 0), PARTS[part], :].astype(jnp.float32)
        return jnp.where(layer >= 0, value, 0.0)

    load_grad.wait()
    pl.semaphore_wait(barrier, 29)

    def length_of(direction, slot, part):
        return 4 - (direction + slot + part) % 2

    def chain_copy(direction, slot, part, step):
        index = direction * 2 + slot
        at = index * STEPS + step
        source = first_ref.at[index] if step == 0 else chain_ref.at[at - 1]
        target = mod8(x + 1) if direction == 0 else mod8(x + 7)
        rows = PARTS[part]
        if step < length_of(direction, slot, part) - 1:
            to_core, into, arrived = core, chain_ref.at[at, rows, :], chain_recv.at[at * 2 + part]
        else:
            to_core, into, arrived = slot, last_ref.at[core, direction, rows, :], last_recv.at[core, direction, part]
        return pltpu.make_async_remote_copy(
            src_ref=source.at[rows, :],
            dst_ref=into,
            send_sem=chain_send.at[at * 2 + part],
            recv_sem=arrived,
            device_id=device(y, z, to_core, target),
            device_id_type=MESH,
        )

    def last_arrival(from_core, direction, part):
        rows = PARTS[part]
        pltpu.make_async_remote_copy(
            src_ref=first_ref.at[0, rows, :],
            dst_ref=last_ref.at[from_core, direction, rows, :],
            send_sem=chain_send.at[part],
            recv_sem=last_recv.at[from_core, direction, part],
            device_id=device(y, z, core, mod8(x + 1)),
            device_id_type=MESH,
        ).wait_recv()

    def advance(slot, step, parts=(0, 1)):
        for part in parts:
            for direction in (1, 0):
                length = length_of(direction, slot, part)
                if step >= length:
                    continue
                ahead = length - step if direction == 0 else step - length
                index = direction * 2 + slot
                if step == 0:
                    first_ref[index, PARTS[part], :] = share(ahead, slot, part)
                else:
                    chain_copy(direction, slot, part, step - 1).wait_recv()
                    at = index * STEPS + step - 1
                    chain_ref[at, PARTS[part], :] = chain_ref[at, PARTS[part], :] + share(ahead, slot, part)
                copy = chain_copy(direction, slot, part, step)
                copy.start()
                started.append(copy)

    def to_sibling(source, target, index):
        return pltpu.make_async_remote_copy(
            src_ref=source,
            dst_ref=target,
            send_sem=pair_send.at[index],
            recv_sem=pair_recv.at[index],
            device_id=device(y, z, 1 - core, x),
            device_id_type=MESH,
        )

    base = to_sibling(base_out_ref, base_ref, 0)
    back = to_sibling(back_out_ref, back_ref, 1)

    def send_base():
        for part in range(2):
            rows = PARTS[part]
            own = share(0, 1 - core, part)
            fresh = momentum_rate * momentum_ref[1 - core, rows, :] + own
            base_out_ref[rows, :] = own + momentum_rate * fresh
        base.start()

    def finish():
        base.wait_recv()
        for part in range(2):
            rows = PARTS[part]
            for from_core in range(2):
                for direction in range(2):
                    last_arrival(from_core, direction, part)
            chains = last_ref[core, 0, rows, :] + last_ref[core, 1, rows, :]
            total = share(0, core, part) + chains
            fresh = momentum_rate * momentum_ref[core, rows, :] + total
            owned_ref[core, rows, :] = total
            field_ref[rows, :] = total + momentum_rate * fresh
            chains = last_ref[1 - core, 0, rows, :] + last_ref[1 - core, 1, rows, :]
            back_out_ref[rows, :] = chains
            pair_ref[rows, :] = base_ref[rows, :] + (1.0 + momentum_rate) * chains

    row = lax.broadcasted_iota(jnp.int32, (HALF, HALF), 0)
    column = lax.broadcasted_iota(jnp.int32, (HALF, HALF), 1)

    def along(axis, ahead):
        return device(mod8(y + ahead), z, core, x) if axis == 0 else device(y, mod8(z + ahead), core, x)

    where = (y, z)

    def gram_copy(stage, order, ahead):
        axis = 1 - order if stage == 1 else order
        if stage == 0:
            source, target = gram_ref.at[order * 8 + mod8(where[order] + ahead)], early_ref.at[order, ahead - 1]
        elif stage == 1:
            source, target = early_sum_ref.at[order], late_ref.at[order, ahead - 1]
        else:
            source, target = late_sum_ref.at[order], whole_ref.at[order * 8 + where[order]]
        index = (stage * 2 + order) * 7 + ahead - 1
        return pltpu.make_async_remote_copy(
            src_ref=source,
            dst_ref=target,
            send_sem=gram_send.at[index],
            recv_sem=gram_recv.at[index],
            device_id=along(axis, ahead),
            device_id_type=MESH,
        )

    def gram_arrival(stage, order, ahead):
        if stage < 2:
            gram_copy(stage, order, ahead).wait_recv()
            return
        index = (stage * 2 + order) * 7 + ahead - 1
        pltpu.make_async_remote_copy(
            src_ref=late_sum_ref.at[order],
            dst_ref=whole_ref.at[order * 8 + mod8(where[order] - ahead)],
            send_sem=gram_send.at[index],
            recv_sem=gram_recv.at[index],
            device_id=along(order, ahead),
            device_id_type=MESH,
        ).wait_recv()

    def start_gram():
        rows_rows = ((1,), (1,))
        mine = split(field_ref[...])
        gram = product(mine, mine, rows_rows)
        other = split(pair_ref[...])
        gram = gram + product(other, other, rows_rows)
        corner, side, rest = gram[:HALF, :HALF], gram[:HALF, HALF:], gram[HALF:, HALF:]
        folded = jnp.where(row >= column, corner, rest)
        edge = jnp.sum(jnp.where(row == column, rest, 0.0), axis=0, keepdims=True)
        gram_ref[:, :TILE, :] = jnp.concatenate([side, folded], axis=0).reshape(16, TILE, HALF)
        piece = lax.broadcasted_iota(jnp.int32, (16, HALF), 0)
        lane = lax.broadcasted_iota(jnp.int32, (16, HALF), 1)
        gram_ref[:, TILE, :] = jnp.where(lane // 8 == piece, edge, 0.0)
        start_stage(0)

    def start_stage(stage):
        for ahead in FAR_FIRST:
            for order in range(2):
                gram_copy(stage, order, ahead).start()

    started = [base, back]
    for step in range(STEPS):
        for slot in range(CAP):
            advance(slot, step)
        if step == 0:
            load_momentum.wait()
            send_base()
    finish()
    start_gram()
    back.start()
    back.wait_recv()
    for part in range(2):
        rows = PARTS[part]
        owned_ref[1 - core, rows, :] = share(0, 1 - core, part) + back_ref[rows, :]
    store = pltpu.make_async_copy(owned_ref, owned_hbm, load_sem.at[3])
    store.start()

    for stage in range(3):
        for order in range(2):
            for ahead in range(1, 8):
                started.append(gram_copy(stage, order, ahead))

    for order in range(2):
        total = gram_ref[order * 8 + where[order]]
        for ahead in range(1, 8):
            gram_arrival(0, order, ahead)
            total = total + early_ref[order, ahead - 1]
        early_sum_ref[order] = total
    start_stage(1)
    for order in range(2):
        total = early_sum_ref[order]
        for ahead in range(1, 8):
            gram_arrival(1, order, ahead)
            total = total + late_ref[order, ahead - 1]
        late_sum_ref[order] = total
        whole_ref[order * 8 + where[order]] = total
    start_stage(2)
    for order in range(2):
        for ahead in range(1, 8):
            gram_arrival(2, order, ahead)

    blocks = whole_ref[:, :TILE, :].reshape(2 * HALF, HALF)
    edge = jnp.sum(whole_ref[:, TILE, :], axis=0, keepdims=True)
    side, folded = blocks[:HALF], blocks[HALF:]
    flipped = folded.T
    corner = jnp.where(row >= column, folded, flipped)
    rest = jnp.where(row < column, folded, jnp.where(row == column, edge, flipped))
    squares = jnp.sum(jnp.where(row == column, corner + rest, 0.0))
    scale = 1.0 / (jnp.sqrt(jnp.full((1, 1), squares, jnp.float32)) + epsilon)
    gram = jnp.concatenate(
        [jnp.concatenate([corner, side], axis=1), jnp.concatenate([side.T, rest], axis=1)], axis=0
    )
    gram = gram * (scale * scale)
    field = jnp.concatenate([field_ref[...], pair_ref[...]], axis=1) * scale

    for step in range(2):
        gram_split = split(gram)
        square = product(gram_split, gram_split)
        square_split = split(square)
        cube = product(gram_split, square_split)
        mixer = quintic_two * gram + quintic_three * square
        mixed = quintic_one * gram + quintic_two * square + quintic_three * cube
        mixer_split = split(mixer)
        field = quintic_one * field + product(mixer_split, split(field))
        gram = quintic_one * mixed + product(split(mixed), mixer_split)
    gram_split = split(gram)
    bent = product(gram_split, split(field))
    twice = product(gram_split, split(bent))
    result = quintic_one * field + quintic_two * bent + quintic_three * twice

    result_ref[0] = result[:, :COLS]
    result_ref[1] = result[:, COLS:]

    def rows_copy(ahead, other_core):
        target = mod8(x + ahead)
        index = other_core * 8 + ahead
        return pltpu.make_async_remote_copy(
            src_ref=result_ref.at[other_core, pl.ds(pl.multiple_of(target * BLOCK, BLOCK), BLOCK), :],
            dst_ref=rows_ref.at[x * 2 + core],
            send_sem=rows_send.at[index],
            recv_sem=rows_recv.at[index],
            device_id=device(y, z, core if other_core == 0 else 1 - core, target),
            device_id_type=MESH,
        )

    def rows_arrival(ahead, other_core):
        source = mod8(x - ahead)
        from_core = core if other_core == 0 else 1 - core
        index = other_core * 8 + ahead
        pltpu.make_async_remote_copy(
            src_ref=result_ref.at[other_core, pl.ds(0, BLOCK), :],
            dst_ref=rows_ref.at[source * 2 + from_core],
            send_sem=rows_send.at[index],
            recv_sem=rows_recv.at[index],
            device_id=device(y, z, from_core, mod8(x + ahead)),
            device_id_type=MESH,
        ).wait_recv()

    partners = [(ahead, other_core) for ahead in FAR_FIRST for other_core in range(2)] + [(0, 1)]
    for ahead, other_core in partners:
        copy = rows_copy(ahead, other_core)
        copy.start()
        started.append(copy)
    rows_ref[x * 2 + core] = result_ref[0, pl.ds(pl.multiple_of(x * BLOCK, BLOCK), BLOCK), :]
    slots = []
    for layer in range(LAYERS):
        rank = jnp.int32(0)
        for before in range(layer):
            rank = rank + (owners[before] == owners[layer]).astype(jnp.int32)
        slots.append(owners[layer] * CAP + rank)
    for ahead, other_core in partners:
        rows_arrival(ahead, other_core)
    for layer in range(LAYERS):
        update_ref[layer] = rows_ref[slots[layer]]
    store_update = pltpu.make_async_copy(update_ref, update_hbm, load_sem.at[4])
    store_update.start()
    for copy in started:
        copy.wait_send()
    store.wait()
    store_update.wait()


def on_device(grad_partial, momentum, owner):
    f32 = jnp.float32
    chains = 8 * STEPS
    dma = pltpu.SemaphoreType.DMA
    shapes = (
        jax.ShapeDtypeStruct((CAP, ROWS, COLS), f32),
        jax.ShapeDtypeStruct((LAYERS, BLOCK, COLS), f32),
    )
    anywhere = pl.BlockSpec(memory_space=pl.ANY)
    owned, update = pl.pallas_call(
        kernel,
        out_shape=shapes,
        in_specs=[anywhere] * 3,
        out_specs=[anywhere] * 2,
        scratch_shapes=[
            pltpu.SMEM((LAYERS,), jnp.int32),
            pltpu.VMEM((LAYERS, ROWS, COLS), jnp.bfloat16),
            pltpu.VMEM((CAP, ROWS, COLS), f32),
            pltpu.VMEM((4, ROWS, COLS), f32),
            pltpu.VMEM((4 * STEPS, ROWS, COLS), f32),
            pltpu.VMEM((CAP, ROWS, COLS), f32),
            pltpu.VMEM((ROWS, COLS), f32),
            pltpu.VMEM((ROWS, COLS), f32),
            pltpu.VMEM((ROWS, COLS), f32),
            pltpu.VMEM((ROWS, COLS), f32),
            pltpu.VMEM((ROWS, COLS), f32),
            pltpu.VMEM((ROWS, COLS), f32),
            pltpu.VMEM((2, 2, ROWS, COLS), f32),
            pltpu.VMEM((16, PIECE, HALF), f32),
            pltpu.VMEM((2, 7, PIECE, HALF), f32),
            pltpu.VMEM((2, PIECE, HALF), f32),
            pltpu.VMEM((2, 7, PIECE, HALF), f32),
            pltpu.VMEM((2, PIECE, HALF), f32),
            pltpu.VMEM((16, PIECE, HALF), f32),
            pltpu.VMEM((2, ROWS, COLS), f32),
            pltpu.VMEM((OWNERS * CAP, BLOCK, COLS), f32),
            pltpu.VMEM((LAYERS, BLOCK, COLS), f32),
            dma((5,)),
            dma((chains,)),
            dma((chains,)),
            dma((2, 2, 2)),
            dma((2,)),
            dma((2,)),
            dma((42,)),
            dma((42,)),
            dma((16,)),
            dma((16,)),
        ],
        compiler_params=pltpu.CompilerParams(
            collective_id=0, has_side_effects=True, vmem_limit_bytes=63 * 1024 * 1024
        ),
    )(owner, grad_partial, momentum)
    return momentum_rate * momentum + owned, update_gain * math.sqrt(N) * update


def solution(mesh):
    placed = (P("expert", None, None, "dp"), P("expert", None, "dp"), P())
    return jax.shard_map(
        on_device,
        mesh=mesh,
        in_specs=placed,
        out_specs=(P("expert", None, "dp"), P(None, "expert", "dp")),
        check_vma=False,
    )
```

time: 78.2 us -> 75.4 us (0.964)
  Pallas kernels: 74.9 us -> 72.1 us
  other arithmetic: 0 us -> 2.42 us
  local copies, waits for them, and re-layouts: 2.39 us -> 0.01 us
    pallas_call x1, Pallas kernels: 74.9 us -> 72.1 us  [on_device(): pl.pallas_call(kernel, out_shape=shapes, in_specs=[anywhere] * 3, out_spe...]
    unnamed x4, local copies, waits for them, and re-layouts: 2.39 us -> 0.01 us
    add x0 -> x1, other arithmetic: none -> 1.72 us  [on_device(): momentum_rate * momentum + owned]
where the time goes in v2:
time: 75.4 us; the launch traced here: 75.2 us
  Pallas kernels  72.1 us (96%)
  other arithmetic  2.42 us (3%)
    pallas_call x1, Pallas kernels, on_device(): pl.pallas_call(kernel, out_shape=shapes, in_specs=[anywhere] * 3, out_spe...  72.1 us
    add x1, other arithmetic, on_device(): momentum_rate * momentum + owned  1.72 us

profile of v2, /device:TPU:1, one launch (start us, length us, event | category | flops | bytes accessed | tf_op | source)
XLA Modules:
  0.0 75.2 jit_solution(5913832401941680920)
XLA Ops:
  0.6 0.0 copy-start
  0.6 72.1 %shard_map.50 = (f32[2,256,128]{2,1,0:T(8,128)}, f32[12,32,128]{2,1,0:T(8,128)}) custom-call(s32[12]{0:T(128)} %owner_hbm.1, bf16[1,12,256,128]{3,2,1,0:T(8,128)(2,1)} %grad_hbm.1, f32[2,256,128]{2,1,0:T(8,128)} %momentum_hbm.1), custom_call_target="tpu_custom_call" | custom-call | tf_op jit(solution)/shard_map/pallas_call | solution.py:421
  72.8 0.0 copy-done
  72.8 0.0 copy-start.1
  72.8 1.7 %multiply_add_fusion = f32[2,256,128]{2,1,0:T(8,128)} fusion(f32[2,256,128]{2,1,0:T(8,128)} %get-tuple-element.4, f32[2,256,128]{2,1,0:T(8,128)S(1)} %copy-done), kind=kLoop, calls=%fused_computation | loop fusion | flops 131072 | bytes 786432 | tf_op jit(solution)/shard_map/add | solution.py:464
  74.5 0.0 copy-done.1
  74.5 0.7 broadcast_multiply_fusion
Async XLA Ops:
  0.6 72.2 %copy-start = (f32[2,256,128]{2,1,0:T(8,128)S(1)}, f32[2,256,128]{2,1,0:T(8,128)}, u32[]{:S(2)}) copy-start(f32[2,256,128]{2,1,0:T(8,128)} %momentum_hbm.1) | copy-start | bytes 786436
  72.8 1.7 %copy-start.1 = (f32[12,32,128]{2,1,0:T(8,128)S(1)}, f32[12,32,128]{2,1,0:T(8,128)}, u32[]{:S(2)}) copy-start(f32[12,32,128]{2,1,0:T(8,128)} %get-tuple-element.5) | copy-start | bytes 589828

commit v3 on v2

--- a/solution.py
+++ b/solution.py
@@ -55,14 +55,14 @@
     owner_hbm,
     grad_hbm,
     momentum_hbm,
-    owned_hbm,
-    update_hbm,
+    new_momentum_hbm,
+    rows_ref,
     owner_ref,
     grad_ref,
     momentum_ref,
     first_ref,
     chain_ref,
-    owned_ref,
+    fresh_ref,
     field_ref,
     pair_ref,
     base_out_ref,
@@ -77,8 +77,6 @@
     late_sum_ref,
     whole_ref,
     result_ref,
-    rows_ref,
-    update_ref,
     load_sem,
     chain_send,
     chain_recv,
@@ -221,7 +219,7 @@
             chains = last_ref[core, 0, rows, :] + last_ref[core, 1, rows, :]
             total = share(0, core, part) + chains
             fresh = momentum_rate * momentum_ref[core, rows, :] + total
-            owned_ref[core, rows, :] = total
+            fresh_ref[core, rows, :] = fresh
             field_ref[rows, :] = total + momentum_rate * fresh
             chains = last_ref[1 - core, 0, rows, :] + last_ref[1 - core, 1, rows, :]
             back_out_ref[rows, :] = chains
@@ -300,8 +298,9 @@
     back.wait_recv()
     for part in range(2):
         rows = PARTS[part]
-        owned_ref[1 - core, rows, :] = share(0, 1 - core, part) + back_ref[rows, :]
-    store = pltpu.make_async_copy(owned_ref, owned_hbm, load_sem.at[3])
+        total = share(0, 1 - core, part) + back_ref[rows, :]
+        fresh_ref[1 - core, rows, :] = momentum_rate * momentum_ref[1 - core, rows, :] + total
+    store = pltpu.make_async_copy(fresh_ref, new_momentum_hbm, load_sem.at[3])
     store.start()
 
     for stage in range(3):
@@ -355,7 +354,8 @@
     gram_split = split(gram)
     bent = product(gram_split, split(field))
     twice = product(gram_split, split(bent))
-    result = quintic_one * field + quintic_two * bent + quintic_three * twice
+    gain = update_gain * math.sqrt(N)
+    result = (gain * quintic_one) * field + (gain * quintic_two) * bent + (gain * quintic_three) * twice
 
     result_ref[0] = result[:, :COLS]
     result_ref[1] = result[:, COLS:]
@@ -390,37 +390,58 @@
         copy = rows_copy(ahead, other_core)
         copy.start()
         started.append(copy)
-    rows_ref[x * 2 + core] = result_ref[0, pl.ds(pl.multiple_of(x * BLOCK, BLOCK), BLOCK), :]
+    keep = pltpu.make_async_copy(
+        result_ref.at[0, pl.ds(pl.multiple_of(x * BLOCK, BLOCK), BLOCK), :], rows_ref.at[x * 2 + core], load_sem.at[4]
+    )
+    keep.start()
+    for ahead, other_core in partners:
+        rows_arrival(ahead, other_core)
+    for copy in started:
+        copy.wait_send()
+    store.wait()
+    keep.wait()
+
+
+def hand_over(
+    owner_hbm, fresh_hbm, rows_hbm, new_momentum_hbm, update_hbm, owner_ref, fresh_ref, rows_ref, update_ref, sems
+):
+    load_rows = pltpu.make_async_copy(rows_hbm, rows_ref, sems.at[0])
+    load_fresh = pltpu.make_async_copy(fresh_hbm, fresh_ref, sems.at[1])
+    load_owner = pltpu.make_async_copy(owner_hbm, owner_ref, sems.at[4])
+    load_owner.start()
+    load_rows.start()
+    load_fresh.start()
+    load_owner.wait()
+    owners = [owner_ref[layer] for layer in range(LAYERS)]
     slots = []
     for layer in range(LAYERS):
         rank = jnp.int32(0)
         for before in range(layer):
             rank = rank + (owners[before] == owners[layer]).astype(jnp.int32)
         slots.append(owners[layer] * CAP + rank)
-    for ahead, other_core in partners:
-        rows_arrival(ahead, other_core)
+    load_rows.wait()
     for layer in range(LAYERS):
         update_ref[layer] = rows_ref[slots[layer]]
-    store_update = pltpu.make_async_copy(update_ref, update_hbm, load_sem.at[4])
+    store_update = pltpu.make_async_copy(update_ref, update_hbm, sems.at[2])
     store_update.start()
-    for copy in started:
-        copy.wait_send()
-    store.wait()
+    load_fresh.wait()
+    store_fresh = pltpu.make_async_copy(fresh_ref, new_momentum_hbm, sems.at[3])
+    store_fresh.start()
     store_update.wait()
+    store_fresh.wait()
 
 
 def on_device(grad_partial, momentum, owner):
     f32 = jnp.float32
     chains = 8 * STEPS
     dma = pltpu.SemaphoreType.DMA
-    shapes = (
-        jax.ShapeDtypeStruct((CAP, ROWS, COLS), f32),
-        jax.ShapeDtypeStruct((LAYERS, BLOCK, COLS), f32),
-    )
+    fresh = jax.ShapeDtypeStruct((CAP, ROWS, COLS), f32)
+    rows = jax.ShapeDtypeStruct((OWNERS * CAP, BLOCK, COLS), f32)
+    update = jax.ShapeDtypeStruct((LAYERS, BLOCK, COLS), f32)
     anywhere = pl.BlockSpec(memory_space=pl.ANY)
-    owned, update = pl.pallas_call(
+    held = pl.pallas_call(
         kernel,
-        out_shape=shapes,
+        out_shape=(fresh, rows),
         in_specs=[anywhere] * 3,
         out_specs=[anywhere] * 2,
         scratch_shapes=[
@@ -444,8 +465,6 @@
             pltpu.VMEM((2, PIECE, HALF), f32),
             pltpu.VMEM((16, PIECE, HALF), f32),
             pltpu.VMEM((2, ROWS, COLS), f32),
-            pltpu.VMEM((OWNERS * CAP, BLOCK, COLS), f32),
-            pltpu.VMEM((LAYERS, BLOCK, COLS), f32),
             dma((5,)),
             dma((chains,)),
             dma((chains,)),
@@ -461,7 +480,20 @@
             collective_id=0, has_side_effects=True, vmem_limit_bytes=63 * 1024 * 1024
         ),
     )(owner, grad_partial, momentum)
-    return momentum_rate * momentum + owned, update_gain * math.sqrt(N) * update
+    return pl.pallas_call(
+        hand_over,
+        out_shape=(fresh, update),
+        in_specs=[anywhere] * 3,
+        out_specs=[anywhere] * 2,
+        scratch_shapes=[
+            pltpu.SMEM((LAYERS,), jnp.int32),
+            pltpu.VMEM((CAP, ROWS, COLS), f32),
+            pltpu.VMEM((OWNERS * CAP, BLOCK, COLS), f32),
+            pltpu.VMEM((LAYERS, BLOCK, COLS), f32),
+            dma((5,)),
+        ],
+        compiler_params=pltpu.CompilerParams(vmem_limit_bytes=63 * 1024 * 1024),
+    )(owner, *held)
 
 
 def solution(mesh):

time: 75.4 us -> 74.2 us (0.984)
  other arithmetic: 2.42 us -> 0 us
  Pallas kernels: 72.1 us -> 73.4 us
    add x1 -> x0, other arithmetic: 1.72 us -> none  [on_device(): momentum_rate * momentum + owned]
    pallas_call x1 -> x2, Pallas kernels: 72.1 us -> 73.4 us  [the longest x1 71.6 us: on_device(): pl.pallas_call(kernel, out_shape=(fresh, rows), in_specs=[anywhere] * 3,...]
where the time goes in v3:
time: 74.2 us; the launch traced here: 74.1 us
  Pallas kernels  73.4 us (99%)
    pallas_call x1, Pallas kernels, on_device(): pl.pallas_call(kernel, out_shape=(fresh, rows), in_specs=[anywhere] * 3,...  71.6 us
    pallas_call x1, Pallas kernels, on_device(): pl.pallas_call(hand_over, out_shape=(fresh, update), in_specs=[anywhere]...  1.78 us

profile of v3, /device:TPU:1, one launch (start us, length us, event | category | flops | bytes accessed | tf_op | source)
XLA Modules:
  0.0 74.1 jit_solution(4105995813865998345)
XLA Ops:
  0.6 71.6 %shard_map.50 = (f32[2,256,128]{2,1,0:T(8,128)}, f32[16,32,128]{2,1,0:T(8,128)}) custom-call(s32[12]{0:T(128)} %owner_hbm.3, bf16[1,12,256,128]{3,2,1,0:T(8,128)(2,1)} %grad_hbm.1, f32[2,256,128]{2,1,0:T(8,128)} %momentum_hbm.1), custom_call_target="tpu_custom_call" | custom-call | tf_op jit(solution)/shard_map/pallas_call | solution.py:442
  72.3 1.8 %shard_map.51 = (f32[2,256,128]{2,1,0:T(8,128)}, f32[12,32,128]{2,1,0:T(8,128)}) custom-call(s32[12]{0:T(128)} %owner_hbm.3, f32[2,256,128]{2,1,0:T(8,128)} %get-tuple-element.4.fresh_hbm, f32[16,32,128]{2,1,0:T(8,128)} %get-tuple-element.5.rows_hbm), custom_call_target="tpu_custom_call" | custom-call | tf_op jit(solution)/shard_map/pallas_call | solution.py:483

commit v4 on v3

--- a/solution.py
+++ b/solution.py
@@ -352,13 +352,7 @@
         field = quintic_one * field + product(mixer_split, split(field))
         gram = quintic_one * mixed + product(split(mixed), mixer_split)
     gram_split = split(gram)
-    bent = product(gram_split, split(field))
-    twice = product(gram_split, split(bent))
     gain = update_gain * math.sqrt(N)
-    result = (gain * quintic_one) * field + (gain * quintic_two) * bent + (gain * quintic_three) * twice
-
-    result_ref[0] = result[:, :COLS]
-    result_ref[1] = result[:, COLS:]
 
     def rows_copy(ahead, other_core):
         target = mod8(x + ahead)
@@ -385,11 +379,16 @@
             device_id_type=MESH,
         ).wait_recv()
 
+    for other_core in (1, 0):
+        columns = field[:, other_core * COLS : (other_core + 1) * COLS]
+        bent = product(gram_split, split(columns))
+        twice = product(gram_split, split(bent))
+        result_ref[other_core] = gain * (quintic_one * columns + quintic_two * bent + quintic_three * twice)
+        for ahead in FAR_FIRST + ((0,) if other_core == 1 else ()):
+            copy = rows_copy(ahead, other_core)
+            copy.start()
+            started.append(copy)
     partners = [(ahead, other_core) for ahead in FAR_FIRST for other_core in range(2)] + [(0, 1)]
-    for ahead, other_core in partners:
-        copy = rows_copy(ahead, other_core)
-        copy.start()
-        started.append(copy)
     keep = pltpu.make_async_copy(
         result_ref.at[0, pl.ds(pl.multiple_of(x * BLOCK, BLOCK), BLOCK), :], rows_ref.at[x * 2 + core], load_sem.at[4]
     )

time: 74.2 us -> 73.6 us (level)
  no operation moved by 1% of the time
where the time goes in v4:
time: 73.6 us; the launch traced here: 73.4 us
  Pallas kernels  72.7 us (99%)
    pallas_call x1, Pallas kernels, on_device(): pl.pallas_call(kernel, out_shape=(fresh, rows), in_specs=[anywhere] * 3,...  71 us
    pallas_call x1, Pallas kernels, on_device(): pl.pallas_call(hand_over, out_shape=(fresh, update), in_specs=[anywhere]...  1.78 us

profile of v4, /device:TPU:1, one launch (start us, length us, event | category | flops | bytes accessed | tf_op | source)
XLA Modules:
  0.0 73.4 jit_solution(5721447472574174275)
XLA Ops:
  0.6 71.0 %shard_map.50 = (f32[2,256,128]{2,1,0:T(8,128)}, f32[16,32,128]{2,1,0:T(8,128)}) custom-call(s32[12]{0:T(128)} %owner_hbm.3, bf16[1,12,256,128]{3,2,1,0:T(8,128)(2,1)} %grad_hbm.1, f32[2,256,128]{2,1,0:T(8,128)} %momentum_hbm.1), custom_call_target="tpu_custom_call" | custom-call | tf_op jit(solution)/shard_map/pallas_call | solution.py:441
  71.6 1.8 %shard_map.51 = (f32[2,256,128]{2,1,0:T(8,128)}, f32[12,32,128]{2,1,0:T(8,128)}) custom-call(s32[12]{0:T(128)} %owner_hbm.3, f32[2,256,128]{2,1,0:T(8,128)} %get-tuple-element.4.fresh_hbm, f32[16,32,128]{2,1,0:T(8,128)} %get-tuple-element.5.rows_hbm), custom_call_target="tpu_custom_call" | custom-call | tf_op jit(solution)/shard_map/pallas_call | solution.py:482
